TPU v7x, 32 devices: a whole 2x2x4 slice. The times are simulated.
32 devices in a mesh: groups: 2 (over x), ctx: 16 (over z, y, core).
Axes of the slice: x: 2, y: 2, z: 4, core: 2. Of those that a mesh axis runs over, the one named last changes fastest.
Arguments:
- queries: bfloat16 [4096, 64, 128], P(('groups', 'ctx')), parts along dimension 0, may hold values from -5 to 5
- head_weights: float32 [4096, 64], P(('groups', 'ctx')), parts along dimension 0, may hold values from -2.5 to 2.5
- keys: bfloat16 [8192, 128], P(('groups', 'ctx')), parts along dimension 0, may hold values from -5 to 5
- targets: float32 [4096, 2048], P(('groups', 'ctx')), parts along dimension 0, may hold values from 0.001 to 1
- block_lists: int32 [64, 32], P(('groups', 'ctx')), parts along dimension 0, may hold values from -1 to 63, as said below
Outputs:
- grad_queries: bfloat16 [4096, 64, 128], P(('groups', 'ctx')), parts along dimension 0
- grad_weights: float32 [4096, 64], P(('groups', 'ctx')), parts along dimension 0
- grad_keys: bfloat16 [8192, 128], P(('groups', 'ctx')), parts along dimension 0
There are 2 independent parts, one for each index of `groups`. A program takes and returns all parts, laid end to end along the dimension named above; each array names one. Nothing has to cross between parts.
Inputs may be any that keep to these rules, and one draw needn't show every extreme that they name: `block_lists`: row c names distinct blocks, none after b(c). Entry 0 is b(c), entries 1 and 2 are blocks 0 and 1; the named blocks come first and -1 fills the rest; some rows name 32 blocks. Over the 2 rows of one device, the blocks named from any one other device (a run of 4 blocks) number at most 2 distinct, blocks 0 and 1 included; every device other than the first reads exactly 2 from the first device.
All inputs are finite; a program needn't handle non-finite values.
Results may differ from a plain program's by a relative error of at most 0.0048.
Values may be sent and summed in bfloat16 or wider, within the bound.
A program may use at most 128 MiB of HBM per device.

v0:
```python
import math

import jax
import jax.numpy as jnp
from jax import lax
from jax.sharding import PartitionSpec as P

BLK = 64


loss_weight = 256.0


def causal_mask(entries, own_block):
    usable = entries >= 0
    clamped = jnp.where(usable, entries, 0)
    offsets = jnp.arange(BLK, dtype=jnp.int32)
    key_pos = (clamped[:, None] * BLK + offsets[None, :]).reshape(-1)
    key_ok = jnp.broadcast_to(usable[:, None], (entries.shape[0], BLK)).reshape(-1)
    query_pos = own_block * BLK + offsets
    return key_ok[None, :] & (key_pos[None, :] <= query_pos[:, None])


def query_block_grads(queries, weights, key_rows, targets, allowed):
    row_count = queries.shape[0]
    head_count = queries.shape[1]
    key_count = key_rows.shape[0]
    key_width = key_rows.shape[1]
    block_width = min(512, key_count)
    groups = key_count // block_width
    inv_root = 1.0 / math.sqrt(key_width)
    key_groups = key_rows.reshape(groups, block_width, key_width)

    def scores(key_block):
        return (
            jnp.einsum("thd,ud->thu", queries, key_block, preferred_element_type=jnp.float32)
            * inv_root
        )

    def index_part(key_block):
        return jnp.sum(weights[:, :, None] * jax.nn.relu(scores(key_block)), axis=1)

    index_score = lax.map(index_part, key_groups)
    index_score = jnp.transpose(index_score, (1, 0, 2)).reshape(row_count, key_count)
    logits = jnp.where(allowed, index_score, -jnp.inf)
    row_peak = jnp.max(logits, axis=1, keepdims=True)
    raised = jnp.exp(logits - row_peak)
    predicted = raised / jnp.sum(raised, axis=1, keepdims=True)
    masked = jnp.where(allowed, targets, 0.0)
    target_prob = masked / jnp.sum(masked, axis=1, keepdims=True)
    logit_grad = (predicted - target_prob) * loss_weight
    grad_parts = jnp.transpose(logit_grad.reshape(row_count, groups, block_width), (1, 0, 2))

    def backward(running, pieces):
        key_block, grad_part = pieces
        grad_q, grad_w = running
        head_score = scores(key_block)
        grad_w = grad_w + jnp.sum(grad_part[:, None, :] * jax.nn.relu(head_score), axis=2)
        mixed = jnp.where(
            head_score > 0, grad_part[:, None, :] * weights[:, :, None] * inv_root, 0.0
        ).astype(jnp.bfloat16)
        grad_q = grad_q + jnp.einsum(
            "thu,ud->thd", mixed, key_block, preferred_element_type=jnp.float32
        )
        grad_k = jnp.einsum("thu,thd->ud", mixed, queries, preferred_element_type=jnp.float32)
        return ((grad_q, grad_w), grad_k)

    start_state = (
        jnp.zeros((row_count, head_count, key_width), jnp.float32),
        jnp.zeros((row_count, head_count), jnp.float32),
    )
    (grad_q, grad_w), grad_k = lax.scan(backward, start_state, (key_groups, grad_parts))
    return (grad_q.astype(jnp.bfloat16), grad_w, grad_k.reshape(key_count, key_width))


def shards(queries, head_weights, keys, targets, block_lists):
    members = lax.axis_size("ctx")
    myself = lax.axis_index("ctx")
    blocks_here = block_lists.shape[0]
    own_count = keys.shape[0] // BLK
    key_width = keys.shape[1]
    head_count = queries.shape[1]
    first_block = myself * own_count + own_count - blocks_here
    usable = block_lists >= 0
    clamped = jnp.where(usable, block_lists, 0)
    everyone = lax.all_gather(keys, "ctx", axis=0, tiled=True)
    key_table = everyone.reshape(members * own_count, BLK, key_width)

    def per_block(grad_table, inputs_now):
        query_rows, weight_rows, target_rows, entries, rows_source, own_block = inputs_now
        key_rows = key_table[rows_source].reshape(-1, key_width)
        allowed = causal_mask(entries, own_block)
        grad_q, grad_w, grad_k = query_block_grads(
            query_rows, weight_rows, key_rows, target_rows, allowed
        )
        grad_table = grad_table.at[rows_source].add(grad_k.reshape(-1, BLK, key_width))
        return (grad_table, (grad_q, grad_w))

    inputs_all = (
        queries.reshape(blocks_here, BLK, head_count, key_width),
        head_weights.reshape(blocks_here, BLK, head_count),
        targets.reshape(blocks_here, BLK, -1),
        block_lists,
        clamped,
        first_block + jnp.arange(blocks_here, dtype=jnp.int32),
    )
    grad_table, (grad_q, grad_w) = lax.scan(
        per_block, jnp.zeros(key_table.shape, jnp.float32), inputs_all
    )
    grad_queries = grad_q.reshape(queries.shape)
    grad_weights = grad_w.reshape(head_weights.shape)
    summed = lax.psum_scatter(
        grad_table.reshape(-1, key_width), "ctx", scatter_dimension=0, tiled=True
    )
    return (grad_queries, grad_weights, summed.astype(jnp.bfloat16))


def solution(mesh):
    in_specs = (
        P(("groups", "ctx"), None, None),
        P(("groups", "ctx"), None),
        P(("groups", "ctx"), None),
        P(("groups", "ctx"), None),
        P(("groups", "ctx"), None),
    )
    out_specs = (
        P(("groups", "ctx"), None, None),
        P(("groups", "ctx"), None),
        P(("groups", "ctx"), None),
    )
    return jax.shard_map(shards, mesh=mesh, in_specs=in_specs, out_specs=out_specs, check_vma=False)
```

profile of v0, /device:TPU:0, one launch (start us, length us, event | category | flops | bytes accessed | tf_op | source)
XLA Modules:
  0.0 274.9 jit_solution(9218499261725989624)
XLA Ops:
  9.5 41.3 %all-gather.2.cloned.1.call-done = bf16[4096,128]{1,0:T(8,128)(2,1)} async-done(((bf16[256,128]{1,0:T(8,128)(2,1)}), bf16[4096,128]{1,0:T(8,128)(2,1)}) %all-gather.2.cloned.1.call-update) | async-done | bytes 1048592 | tf_op jit(solution)/shard_map/all_gather | solution.py:86
  52.4 153.7 %while.41 = (s32[]{:T(128)}, f32[64,64,128]{2,1,0:T(8,128)}, bf16[2,64,64,128]{3,2,1,0:T(8,128)(2,1)}, f32[2,64,64]{2,1,0:T(8,128)S(1)}, s32[2,32]{1,0:T(2,128)S...) while((s32[]{:T(128)}, f32[64,64,128]{2,1,0:T(8,128)}, ...), condition=%wide.region_11.12_spmd, body=%wide.region_0.11_spmd.sunk | while | flops 2194121984 | bytes 70268824 | solution.py:107
  62.0 2.3 fusion.39
  64.3 16.6 %while.42 = (s32[]{:T(128)}, f32[4,64,512]{2,0,1:T(4,128)S(1)}, f32[64,64]{1,0:T(8,128)S(1)}, bf16[4,512,128]{2,1,0:T(8,128)(2,1)S(1)}, bf16[64,64,128]{2,1,0:T(8,128)(2,1)}, /*index=5*/s32[]{:T(128)}, s32[]{:T(128)}) while((s32[]{:T(128)}, f32[4,64,512]{2,0,1:T(4,128)S(1)}, f32[64,64]{1,0:T(8,128)S(1)}, bf16[4,512,128]{2,1,0:T(8,128)(2,1)S(1)}, ...), condition=%wide.region_3.3_spmd, body=%wide.region_1.2_spmd.sunk | while | flops 545226752 | bytes 1867869 | solution.py:43
  64.3 2.7 multiply_reduce_fusion.2
  68.5 2.7 multiply_reduce_fusion.2
  72.7 2.7 multiply_reduce_fusion.2
  76.8 2.7 multiply_reduce_fusion.2
  83.6 37.2 %while.43 = (s32[]{:T(128)}, f32[64,64,128]{2,1,0:T(8,128)}, f32[64,64]{1,0:T(8,128)S(1)}, f32[4,512,128]{2,1,0:T(8,128)}, bf16[4,512,128]{2,1,0:T(8,128)(2,1)S(...) while((s32[]{:T(128)}, f32[64,64,128]{2,1,0:T(8,128)}, ...), condition=%wide.region_9.9_spmd.clone, body=%wide.region_7.8_spmd.clone.sunk | while | flops 1645219840 | bytes 49791164 | solution.py:72
  85.9 4.0 %fusion.48 = f32[4,512,128]{2,1,0:T(8,128)} fusion(f32[4,512,128]{2,1,0:T(8,128)} %get-tuple-element.468, s32[]{:T(128)S(6)} %copy.62, bf16[64,64,128]{2,0,1:T(8,128)(2,1)S(1)} %get-tuple-element.480, f32[512,64,64]{0,2,1:T(8,128)S(1)} %get-tuple-element.432, f32[64,64]{1,0:T(8,128)S(1)} %get-tuple-element.482, f32[64,512]{1,0:T(8,128)S(1)} %bitcast.138), kind=kOutput, calls=%fused_computation.11.clone.1 | convolution fusion | flops 549453824 | bytes 9846788 | tf_op jit(solution)/shard_map/while/body/eval_jaxpr/while/body/eval_jaxpr/thu,thd->ud/dot_general | solution.py:65
  93.1 2.1 fusion.47
  95.2 4.0 %fusion.48 = f32[4,512,128]{2,1,0:T(8,128)} fusion(f32[4,512,128]{2,1,0:T(8,128)} %get-tuple-element.468, s32[]{:T(128)S(6)} %copy.62, bf16[64,64,128]{2,0,1:T(8,128)(2,1)S(1)} %get-tuple-element.480, f32[512,64,64]{0,2,1:T(8,128)S(1)} %get-tuple-element.432, f32[64,64]{1,0:T(8,128)S(1)} %get-tuple-element.482, f32[64,512]{1,0:T(8,128)S(1)} %bitcast.138), kind=kOutput, calls=%fused_computation.11.clone.1 | convolution fusion | flops 549453824 | bytes 9846788 | tf_op jit(solution)/shard_map/while/body/eval_jaxpr/while/body/eval_jaxpr/thu,thd->ud/dot_general | solution.py:65
  102.4 2.1 fusion.47
  104.5 4.0 %fusion.48 = f32[4,512,128]{2,1,0:T(8,128)} fusion(f32[4,512,128]{2,1,0:T(8,128)} %get-tuple-element.468, s32[]{:T(128)S(6)} %copy.62, bf16[64,64,128]{2,0,1:T(8,128)(2,1)S(1)} %get-tuple-element.480, f32[512,64,64]{0,2,1:T(8,128)S(1)} %get-tuple-element.432, f32[64,64]{1,0:T(8,128)S(1)} %get-tuple-element.482, f32[64,512]{1,0:T(8,128)S(1)} %bitcast.138), kind=kOutput, calls=%fused_computation.11.clone.1 | convolution fusion | flops 549453824 | bytes 9846788 | tf_op jit(solution)/shard_map/while/body/eval_jaxpr/while/body/eval_jaxpr/thu,thd->ud/dot_general | solution.py:65
  113.8 4.0 %fusion.48 = f32[4,512,128]{2,1,0:T(8,128)} fusion(f32[4,512,128]{2,1,0:T(8,128)} %get-tuple-element.468, s32[]{:T(128)S(6)} %copy.62, bf16[64,64,128]{2,0,1:T(8,128)(2,1)S(1)} %get-tuple-element.480, f32[512,64,64]{0,2,1:T(8,128)S(1)} %get-tuple-element.432, f32[64,64]{1,0:T(8,128)S(1)} %get-tuple-element.482, f32[64,512]{1,0:T(8,128)S(1)} %bitcast.138), kind=kOutput, calls=%fused_computation.11.clone.1 | convolution fusion | flops 549453824 | bytes 9846788 | tf_op jit(solution)/shard_map/while/body/eval_jaxpr/while/body/eval_jaxpr/thu,thd->ud/dot_general | solution.py:65
  120.9 2.8 %bitcast_dynamic-update-slice_fusion.4 = bf16[2,64,64,128]{3,2,1,0:T(8,128)(2,1)} fusion(bf16[2,64,64,128]{3,2,1,0:T(8,128)(2,1)} %get-tuple-element.505, s32[]{:T(128)S(6)} %copy.77, f32[64,64,128]{2,1,0:T(8,128)} %get-tuple-element.415), kind=kLoop, calls=%fused_computation.25.clone.1 | loop fusion | flops 524288 | bytes 3145732 | tf_op jit(solution)/shard_map/while/body/jit(dynamic_update_index_in_dim)/dynamic_update_slice | solution.py:107
  123.6 5.6 %scatter_fusion = f32[64,64,128]{2,1,0:T(8,128)} fusion(f32[64,64,128]{2,1,0:T(8,128)} %get-tuple-element.504, s32[32]{0:T(128)S(1)} %fusion.36, f32[32,64,128]{2,1,0:T(8,128)} %bitcast.144), kind=kCustom, calls=%fused_computation.1.clone.1 | custom fusion | flops 262144 | bytes 3145856 | tf_op jit(solution)/shard_map/while/body/eval_jaxpr/scatter-add | solution.py:96
  138.9 2.3 fusion.39
  141.2 16.6 %while.42 = (s32[]{:T(128)}, f32[4,64,512]{2,0,1:T(4,128)S(1)}, f32[64,64]{1,0:T(8,128)S(1)}, bf16[4,512,128]{2,1,0:T(8,128)(2,1)S(1)}, bf16[64,64,128]{2,1,0:T(8,128)(2,1)}, /*index=5*/s32[]{:T(128)}, s32[]{:T(128)}) while((s32[]{:T(128)}, f32[4,64,512]{2,0,1:T(4,128)S(1)}, f32[64,64]{1,0:T(8,128)S(1)}, bf16[4,512,128]{2,1,0:T(8,128)(2,1)S(1)}, ...), condition=%wide.region_3.3_spmd, body=%wide.region_1.2_spmd.sunk | while | flops 545226752 | bytes 1867869 | solution.py:43
  141.2 2.7 multiply_reduce_fusion.2
  145.3 2.7 multiply_reduce_fusion.2
  149.5 2.7 multiply_reduce_fusion.2
  153.7 2.7 multiply_reduce_fusion.2
  160.5 37.2 %while.43 = (s32[]{:T(128)}, f32[64,64,128]{2,1,0:T(8,128)}, f32[64,64]{1,0:T(8,128)S(1)}, f32[4,512,128]{2,1,0:T(8,128)}, bf16[4,512,128]{2,1,0:T(8,128)(2,1)S(...) while((s32[]{:T(128)}, f32[64,64,128]{2,1,0:T(8,128)}, ...), condition=%wide.region_9.9_spmd.clone, body=%wide.region_7.8_spmd.clone.sunk | while | flops 1645219840 | bytes 49791164 | solution.py:72
  162.7 4.0 %fusion.48 = f32[4,512,128]{2,1,0:T(8,128)} fusion(f32[4,512,128]{2,1,0:T(8,128)} %get-tuple-element.468, s32[]{:T(128)S(6)} %copy.62, bf16[64,64,128]{2,0,1:T(8,128)(2,1)S(1)} %get-tuple-element.480, f32[512,64,64]{0,2,1:T(8,128)S(1)} %get-tuple-element.432, f32[64,64]{1,0:T(8,128)S(1)} %get-tuple-element.482, f32[64,512]{1,0:T(8,128)S(1)} %bitcast.138), kind=kOutput, calls=%fused_computation.11.clone.1 | convolution fusion | flops 549453824 | bytes 9846788 | tf_op jit(solution)/shard_map/while/body/eval_jaxpr/while/body/eval_jaxpr/thu,thd->ud/dot_general | solution.py:65
  172.0 4.0 %fusion.48 = f32[4,512,128]{2,1,0:T(8,128)} fusion(f32[4,512,128]{2,1,0:T(8,128)} %get-tuple-element.468, s32[]{:T(128)S(6)} %copy.62, bf16[64,64,128]{2,0,1:T(8,128)(2,1)S(1)} %get-tuple-element.480, f32[512,64,64]{0,2,1:T(8,128)S(1)} %get-tuple-element.432, f32[64,64]{1,0:T(8,128)S(1)} %get-tuple-element.482, f32[64,512]{1,0:T(8,128)S(1)} %bitcast.138), kind=kOutput, calls=%fused_computation.11.clone.1 | convolution fusion | flops 549453824 | bytes 9846788 | tf_op jit(solution)/shard_map/while/body/eval_jaxpr/while/body/eval_jaxpr/thu,thd->ud/dot_general | solution.py:65
  179.2 2.1 fusion.47
  181.3 4.0 %fusion.48 = f32[4,512,128]{2,1,0:T(8,128)} fusion(f32[4,512,128]{2,1,0:T(8,128)} %get-tuple-element.468, s32[]{:T(128)S(6)} %copy.62, bf16[64,64,128]{2,0,1:T(8,128)(2,1)S(1)} %get-tuple-element.480, f32[512,64,64]{0,2,1:T(8,128)S(1)} %get-tuple-element.432, f32[64,64]{1,0:T(8,128)S(1)} %get-tuple-element.482, f32[64,512]{1,0:T(8,128)S(1)} %bitcast.138), kind=kOutput, calls=%fused_computation.11.clone.1 | convolution fusion | flops 549453824 | bytes 9846788 | tf_op jit(solution)/shard_map/while/body/eval_jaxpr/while/body/eval_jaxpr/thu,thd->ud/dot_general | solution.py:65
  190.6 4.0 %fusion.48 = f32[4,512,128]{2,1,0:T(8,128)} fusion(f32[4,512,128]{2,1,0:T(8,128)} %get-tuple-element.468, s32[]{:T(128)S(6)} %copy.62, bf16[64,64,128]{2,0,1:T(8,128)(2,1)S(1)} %get-tuple-element.480, f32[512,64,64]{0,2,1:T(8,128)S(1)} %get-tuple-element.432, f32[64,64]{1,0:T(8,128)S(1)} %get-tuple-element.482, f32[64,512]{1,0:T(8,128)S(1)} %bitcast.138), kind=kOutput, calls=%fused_computation.11.clone.1 | convolution fusion | flops 549453824 | bytes 9846788 | tf_op jit(solution)/shard_map/while/body/eval_jaxpr/while/body/eval_jaxpr/thu,thd->ud/dot_general | solution.py:65
  197.7 2.8 %bitcast_dynamic-update-slice_fusion.4 = bf16[2,64,64,128]{3,2,1,0:T(8,128)(2,1)} fusion(bf16[2,64,64,128]{3,2,1,0:T(8,128)(2,1)} %get-tuple-element.505, s32[]{:T(128)S(6)} %copy.77, f32[64,64,128]{2,1,0:T(8,128)} %get-tuple-element.415), kind=kLoop, calls=%fused_computation.25.clone.1 | loop fusion | flops 524288 | bytes 3145732 | tf_op jit(solution)/shard_map/while/body/jit(dynamic_update_index_in_dim)/dynamic_update_slice | solution.py:107
  200.5 5.6 %scatter_fusion = f32[64,64,128]{2,1,0:T(8,128)} fusion(f32[64,64,128]{2,1,0:T(8,128)} %get-tuple-element.504, s32[32]{0:T(128)S(1)} %fusion.36, f32[32,64,128]{2,1,0:T(8,128)} %bitcast.144), kind=kCustom, calls=%fused_computation.1.clone.1 | custom fusion | flops 262144 | bytes 3145856 | tf_op jit(solution)/shard_map/while/body/eval_jaxpr/scatter-add | solution.py:96
  206.8 59.7 %reduce-scatter.2.cloned.1.call-done = f32[256,128]{1,0:T(8,128)} async-done(((f32[4096,128]{1,0:T(8,128)}), f32[256,128]{1,0:T(8,128)}) %reduce-scatter.2.cloned.1.call-update) | async-done | bytes 131088 | tf_op jit(solution)/shard_map/reduce_scatter | solution.py:112
  (167 shorter events, 76.6 us)
Async XLA Ops:
  7.2 43.7 %all-gather.2.cloned.1.call-start = ((), (), s32[]{:S(2)}) async-start(), calls=%async_computation.1 | async-start | bytes 1114112 | tf_op jit(solution)/shard_map/all_gather | solution.py:86
  7.9 258.6 %reduce-scatter.2.cloned.1.call-start = ((), (), s32[]{:S(2)}) async-start(), calls=%async_computation.2 | async-start | bytes 2228224 | tf_op jit(solution)/shard_map/reduce_scatter | solution.py:112
  85.9 4.0 %copy-start = (f32[64,64,128]{2,1,0:T(8,128)S(1)}, f32[64,64,128]{2,1,0:T(8,128)}, u32[]{:S(2)}) copy-start(f32[64,64,128]{2,1,0:T(8,128)} %get-tuple-element.466) | copy-start | bytes 6291460 | tf_op jit(solution)/shard_map/while/body/eval_jaxpr/while
  91.6 1.4 copy-start.1
  95.2 4.0 %copy-start = (f32[64,64,128]{2,1,0:T(8,128)S(1)}, f32[64,64,128]{2,1,0:T(8,128)}, u32[]{:S(2)}) copy-start(f32[64,64,128]{2,1,0:T(8,128)} %get-tuple-element.466) | copy-start | bytes 6291460 | tf_op jit(solution)/shard_map/while/body/eval_jaxpr/while
  100.9 1.4 copy-start.1
  104.5 4.0 %copy-start = (f32[64,64,128]{2,1,0:T(8,128)S(1)}, f32[64,64,128]{2,1,0:T(8,128)}, u32[]{:S(2)}) copy-start(f32[64,64,128]{2,1,0:T(8,128)} %get-tuple-element.466) | copy-start | bytes 6291460 | tf_op jit(solution)/shard_map/while/body/eval_jaxpr/while
  110.2 1.4 copy-start.1
  113.8 4.0 %copy-start = (f32[64,64,128]{2,1,0:T(8,128)S(1)}, f32[64,64,128]{2,1,0:T(8,128)}, u32[]{:S(2)}) copy-start(f32[64,64,128]{2,1,0:T(8,128)} %get-tuple-element.466) | copy-start | bytes 6291460 | tf_op jit(solution)/shard_map/while/body/eval_jaxpr/while
  119.5 1.4 copy-start.1
  162.7 4.0 %copy-start = (f32[64,64,128]{2,1,0:T(8,128)S(1)}, f32[64,64,128]{2,1,0:T(8,128)}, u32[]{:S(2)}) copy-start(f32[64,64,128]{2,1,0:T(8,128)} %get-tuple-element.466) | copy-start | bytes 6291460 | tf_op jit(solution)/shard_map/while/body/eval_jaxpr/while
  168.4 1.4 copy-start.1
  172.0 4.0 %copy-start = (f32[64,64,128]{2,1,0:T(8,128)S(1)}, f32[64,64,128]{2,1,0:T(8,128)}, u32[]{:S(2)}) copy-start(f32[64,64,128]{2,1,0:T(8,128)} %get-tuple-element.466) | copy-start | bytes 6291460 | tf_op jit(solution)/shard_map/while/body/eval_jaxpr/while
  177.8 1.4 copy-start.1
  181.3 4.0 %copy-start = (f32[64,64,128]{2,1,0:T(8,128)S(1)}, f32[64,64,128]{2,1,0:T(8,128)}, u32[]{:S(2)}) copy-start(f32[64,64,128]{2,1,0:T(8,128)} %get-tuple-element.466) | copy-start | bytes 6291460 | tf_op jit(solution)/shard_map/while/body/eval_jaxpr/while
  187.1 1.4 copy-start.1
  190.6 4.0 %copy-start = (f32[64,64,128]{2,1,0:T(8,128)S(1)}, f32[64,64,128]{2,1,0:T(8,128)}, u32[]{:S(2)}) copy-start(f32[64,64,128]{2,1,0:T(8,128)} %get-tuple-element.466) | copy-start | bytes 6291460 | tf_op jit(solution)/shard_map/while/body/eval_jaxpr/while
  196.4 1.4 copy-start.1
Sparse Core Ops, SparseCore 0:
  10.2 40.6 all-gather.1
  206.2 60.2 reduce-scatter.1
where the time goes:
time: 276 us; the launch traced here: 275 us
  waiting for transfers between devices  102 us (37%)
  matrix products  84.1 us (30%)
  local copies, waits for them, and re-layouts  43 us (16%)
  other arithmetic  29.9 us (11%)
  between operations  14.1 us (5%)
    reduce_scatter x1, waiting for transfers between devices, shards(): lax.psum_scatter(grad_table.reshape(-1, key_width), 'ctx', scatter_dimens...  59.7 us
    all_gather x1, waiting for transfers between devices, shards(): everyone = lax.all_gather(keys, 'ctx', axis=0, tiled=True)  41.3 us
    dot_general x16, matrix products, scores(): jnp.einsum('thd,ud->thu', queries, key_block, preferred_element_type=jnp....  38.3 us
    dot_general x8, matrix products, backward(): jnp.einsum('thu,thd->ud', mixed, queries, preferred_element_type=jnp.floa...  31.8 us
    dot_general x8, matrix products, backward(): jnp.einsum('thu,ud->thd', mixed, key_block, preferred_element_type=jnp.fl...  14 us
    scatter-add x2, other arithmetic, per_block(): grad_table.at[rows_source].add(grad_k.reshape(-1, BLK, key_width))  11.2 us
    dynamic_update_slice x16, local copies, waits for them, and re-layouts, query_block_grads(): index_score = lax.map(index_part, key_groups)  11.1 us
    while x32, local copies, waits for them, and re-layouts  10.8 us
  transfers between devices with their start and end apart: 2, of which 2 were waited for; matrix products, arithmetic and copies ran while one was open for 1% of the time, Pallas kernels for 0%

commit v1 on v0

v1 whole, which is shorter than its diff:
```python
import functools
import math

import jax
import jax.numpy as jnp
from jax import lax
from jax.experimental import pallas as pl
from jax.experimental.pallas import tpu as pltpu
from jax.sharding import PartitionSpec as P

BLK = 64
LOSS_WEIGHT = 256.0
FAR = 2**30
UC = 256
TF = 8
TB = 8


def compute_kernel(
    lists, q_ref, w_ref, table_ref, targets_ref, gq_ref, gw_ref, gk_ref,
    k_scr, kt_scr, s_scr, wb_scr, idx_scr, g_scr, gkt_scr,
):
    c = pl.program_id(0)
    tokens, heads, width = q_ref.shape
    cand = targets_ref.shape[1]
    entries = cand // BLK
    inv_root = 1.0 / math.sqrt(width)

    @pl.when(c == 0)
    def _():
        gk_ref[...] = jnp.zeros_like(gk_ref)

    for e in range(entries):
        source = jnp.maximum(lists[c, e], 0)
        k_scr[e * BLK : (e + 1) * BLK, :] = table_ref[source]
    kt_scr[...] = k_scr[...].T
    gkt_scr[...] = jnp.zeros_like(gkt_scr)

    for t0 in range(0, tokens, 8):
        wb_scr[t0 : t0 + 8] = jnp.broadcast_to(
            (w_ref[t0 : t0 + 8, :] * inv_root)[:, :, None], (8, heads, width)
        )

    def forward(i, carry):
        t0 = pl.multiple_of(i * TF, TF)
        q = q_ref[pl.ds(t0, TF)].reshape(TF * heads, width)
        for u in range(0, cand, UC):
            s = jnp.dot(q, kt_scr[:, u : u + UC], preferred_element_type=jnp.float32)
            s_scr[pl.ds(t0 * heads, TF * heads), u : u + UC] = s.astype(jnp.bfloat16)
            s = jnp.maximum(s, 0.0).reshape(TF, heads, UC)
            parts = [
                jnp.sum(wb_scr[pl.ds(t0, TF)] * s[:, :, v : v + width], axis=1)
                for v in range(0, UC, width)
            ]
            idx_scr[pl.ds(t0, TF), u : u + UC] = jnp.concatenate(parts, axis=1)
        return carry

    lax.fori_loop(0, tokens // TF, forward, 0)

    lane = lax.broadcasted_iota(jnp.int32, (1, 2 * BLK), 1)
    pieces = []
    for e in range(0, entries, 2):
        low = jnp.where(lists[c, e] >= 0, lists[c, e] * BLK, FAR)
        high = jnp.where(lists[c, e + 1] >= 0, lists[c, e + 1] * BLK - BLK, FAR)
        pieces.append(jnp.where(lane < BLK, low, high) + lane)
    key_pos = jnp.concatenate(pieces, axis=1)
    for t0 in range(0, tokens, 8):
        row = lax.broadcasted_iota(jnp.int32, (8, cand), 0) + (lists[c, 0] * BLK + t0)
        allowed = key_pos <= row
        logits = jnp.where(allowed, idx_scr[t0 : t0 + 8, :], -jnp.inf)
        peak = jnp.max(logits, axis=1, keepdims=True)
        raised = jnp.exp(logits - peak)
        masked = jnp.where(allowed, targets_ref[t0 : t0 + 8, :], 0.0)
        p_scale = LOSS_WEIGHT / jnp.sum(raised, axis=1, keepdims=True)
        t_scale = LOSS_WEIGHT / jnp.sum(masked, axis=1, keepdims=True)
        g_scr[t0 : t0 + 8, :] = raised * p_scale - masked * t_scale

    def backward(i, carry):
        t0 = pl.multiple_of(i * TB, TB)
        rows = TB * heads
        q = q_ref[pl.ds(t0, TB)].astype(jnp.float32)
        wb = wb_scr[pl.ds(t0, TB)]
        wqt = (q * wb).reshape(rows, width).T.astype(jnp.bfloat16)
        gq = jnp.zeros((rows, width), jnp.float32)
        for u in range(0, cand, UC):
            g = g_scr[pl.ds(t0, TB), u : u + UC]
            g = jnp.broadcast_to(g[:, None, :], (TB, 16, UC)).astype(jnp.bfloat16)
            s = s_scr[pl.ds(t0 * heads, rows), u : u + UC].reshape(TB, heads // 16, 16, UC)
            mixed = jnp.where(s > 0, g[:, None], jnp.zeros((), jnp.bfloat16)).reshape(rows, UC)
            gq = gq + jnp.dot(
                mixed, k_scr[u : u + UC, :], preferred_element_type=jnp.float32
            )
            gkt_scr[:, u : u + UC] += jnp.dot(
                wqt, mixed, preferred_element_type=jnp.float32
            )
        gq = gq.reshape(TB, heads, width)
        gq_ref[pl.ds(t0, TB)] = (gq * wb).astype(jnp.bfloat16)
        gw_ref[pl.ds(t0, TB), :] = jnp.sum(gq * q, axis=2) * inv_root
        return carry

    lax.fori_loop(0, tokens // TB, backward, 0)

    for u in range(0, cand, 2 * BLK):
        part = gkt_scr[:, u : u + 2 * BLK].T
        for v in range(2):
            target = jnp.maximum(lists[c, u // BLK + v], 0)
            gk_ref[target] += part[v * BLK : (v + 1) * BLK, :]


def shards(queries, head_weights, keys, targets, block_lists):
    width = keys.shape[1]
    heads = queries.shape[1]
    cand = targets.shape[1]
    blocks_here = block_lists.shape[0]
    everyone = lax.all_gather(keys, "ctx", axis=0, tiled=True)
    total = everyone.shape[0] // BLK
    table = everyone.reshape(total, BLK, width)
    flops = 6 * queries.shape[0] * heads * cand * width
    once = pl.Buffered(1)
    grad_q, grad_w, grad_table = pl.pallas_call(
        compute_kernel,
        grid_spec=pltpu.PrefetchScalarGridSpec(
            num_scalar_prefetch=1,
            grid=(blocks_here,),
            in_specs=[
                pl.BlockSpec((BLK, heads, width), lambda c, lists: (c, 0, 0)),
                pl.BlockSpec((BLK, heads), lambda c, lists: (c, 0)),
                pl.BlockSpec((total, BLK, width), lambda c, lists: (0, 0, 0), pipeline_mode=once),
                pl.BlockSpec((BLK, cand), lambda c, lists: (c, 0)),
            ],
            out_specs=[
                pl.BlockSpec((BLK, heads, width), lambda c, lists: (c, 0, 0)),
                pl.BlockSpec((BLK, heads), lambda c, lists: (c, 0)),
                pl.BlockSpec((total, BLK, width), lambda c, lists: (0, 0, 0), pipeline_mode=once),
            ],
            scratch_shapes=[
                pltpu.VMEM((cand, width), jnp.bfloat16),
                pltpu.VMEM((width, cand), jnp.bfloat16),
                pltpu.VMEM((BLK * heads, cand), jnp.bfloat16),
                pltpu.VMEM((BLK, heads, width), jnp.float32),
                pltpu.VMEM((BLK, cand), jnp.float32),
                pltpu.VMEM((BLK, cand), jnp.float32),
                pltpu.VMEM((width, cand), jnp.float32),
            ],
        ),
        out_shape=[
            jax.ShapeDtypeStruct(queries.shape, jnp.bfloat16),
            jax.ShapeDtypeStruct(head_weights.shape, jnp.float32),
            jax.ShapeDtypeStruct((total, BLK, width), jnp.float32),
        ],
        compiler_params=pltpu.CompilerParams(vmem_limit_bytes=60 * 2**20),
        cost_estimate=pl.CostEstimate(flops=flops, bytes_accessed=10 * 2**20, transcendentals=0),
    )(block_lists, queries, head_weights, table, targets)
    summed = lax.psum_scatter(
        grad_table.reshape(-1, width), "ctx", scatter_dimension=0, tiled=True
    )
    return (grad_q, grad_w, summed.astype(jnp.bfloat16))


def solution(mesh):
    in_specs = (
        P(("groups", "ctx"), None, None),
        P(("groups", "ctx"), None),
        P(("groups", "ctx"), None),
        P(("groups", "ctx"), None),
        P(("groups", "ctx"), None),
    )
    out_specs = (
        P(("groups", "ctx"), None, None),
        P(("groups", "ctx"), None),
        P(("groups", "ctx"), None),
    )
    return jax.shard_map(shards, mesh=mesh, in_specs=in_specs, out_specs=out_specs, check_vma=False)
```

time: 276 us -> 156 us (0.57)
  matrix products: 84.1 us -> 0 us
  local copies, waits for them, and re-layouts: 43 us -> 2.99 us
  Pallas kernels: 0 us -> 36 us
  other arithmetic: 29.9 us -> 1.54 us
    dot_general x32 -> x0, matrix products: 84.1 us -> none  [the longest x16 38.3 us: scores(): jnp.einsum('thd,ud->thu', queries, key_block, preferred_element_type=jnp....]
    pallas_call x0 -> x1, Pallas kernels: none -> 36 us  [shards(): pl.pallas_call(compute_kernel, grid_spec=pltpu.PrefetchScalarGridSpec(num...]
    scatter-add x2 -> x0, other arithmetic: 11.2 us -> none  [per_block(): grad_table.at[rows_source].add(grad_k.reshape(-1, BLK, key_width))]
    dynamic_update_slice x18 -> x0, local copies, waits for them, and re-layouts: 11.1 us -> none  [the longest x16 11.1 us: query_block_grads(): index_score = lax.map(index_part, key_groups)]
    while x32 -> x0, local copies, waits for them, and re-layouts: 10.8 us -> none
    dynamic_slice x24 -> x0, local copies, waits for them, and re-layouts: 7.53 us -> none  [the longest x8 6.52 us: shards(): lax.scan(per_block, jnp.zeros(key_table.shape, jnp.float32), inputs_all)]
    dynamic_update_slice x2 -> x0, other arithmetic: 5.52 us -> none  [shards(): lax.scan(per_block, jnp.zeros(key_table.shape, jnp.float32), inputs_all)]
    squeeze x8 -> x0, local copies, waits for them, and re-layouts: 5.46 us -> none  [shards(): lax.scan(per_block, jnp.zeros(key_table.shape, jnp.float32), inputs_all)]
where the time goes in v1:
time: 156 us
  waiting for transfers between devices  101 us (65%)
  Pallas kernels  36 us (23%)
  between operations  14 us (9%)
  local copies, waits for them, and re-layouts  2.99 us (2%)
    reduce_scatter x1, waiting for transfers between devices, shards(): lax.psum_scatter(grad_table.reshape(-1, width), 'ctx', scatter_dimension=...  59.1 us
    all_gather x1, waiting for transfers between devices, shards(): everyone = lax.all_gather(keys, 'ctx', axis=0, tiled=True)  41.4 us
    pallas_call x1, Pallas kernels, shards(): pl.pallas_call(compute_kernel, grid_spec=pltpu.PrefetchScalarGridSpec(num...  36 us
  transfers between devices with their start and end apart: 2, of which 2 were waited for; matrix products, arithmetic and copies ran while one was open for 1% of the time, Pallas kernels for 0%

profile of v1, /device:TPU:0, one launch (start us, length us, event | category | flops | bytes accessed | tf_op | source)
XLA Modules:
  0.0 155.8 jit_solution(11448179450729769979)
XLA Ops:
  7.2 0.0 all-gather.2.cloned.1.call-start
  7.2 0.7 all-gather.2.cloned.1.call-update
  7.9 0.0 reduce-scatter.2.cloned.1.call-start
  7.9 1.5 copy.8.w_ref
  9.4 41.4 %all-gather.2.cloned.1.call-done = bf16[4096,128]{1,0:T(8,128)(2,1)} async-done(((bf16[256,128]{1,0:T(8,128)(2,1)}), bf16[4096,128]{1,0:T(8,128)(2,1)}) %all-gather.2.cloned.1.call-update) | async-done | bytes 1048592 | tf_op jit(solution)/shard_map/all_gather | solution.py:115
  50.8 36.0 %shard_map.76 = (bf16[128,64,128]{2,1,0:T(8,128)(2,1)}, f32[128,64]{1,0:T(8,128)}, f32[64,64,128]{2,1,0:T(8,128)}) custom-call(s32[2,32]{1,0:T(2,128)} %lists.1, bf16[128,64,128]{2,1,0:T(8,128)(2,1)} %q_ref.1, f32[128,64]{1,0:T(8,128)} %copy.8.w_ref, bf16[64,64,128]{2,1,0:T(8,128)(2,1)} %bitcast.3, f32[128,2048]{1,0:T(8,128)} %targets_ref.1), custom_call_target="tpu_custom_call" | custom-call | flops 12884901888 | bytes 10485760 | tf_op jit(solution)/shard_map/pallas_call | solution.py:120
  86.8 0.0 copy-start
  86.8 0.0 reduce-scatter.2.cloned.1.call-update
  86.8 0.8 copy-done
  87.7 0.7 copy.9
  88.3 59.1 %reduce-scatter.2.cloned.1.call-done = f32[256,128]{1,0:T(8,128)} async-done(((f32[4096,128]{1,0:T(8,128)}), f32[256,128]{1,0:T(8,128)}) %reduce-scatter.2.cloned.1.call-update) | async-done | bytes 131088 | tf_op jit(solution)/shard_map/reduce_scatter | solution.py:154
  147.4 1.5 convert_element_type.3
Async XLA Ops:
  7.2 43.7 %all-gather.2.cloned.1.call-start = ((), (), s32[]{:S(2)}) async-start(), calls=%async_computation.1 | async-start | bytes 1114112 | tf_op jit(solution)/shard_map/all_gather | solution.py:115
  7.9 139.5 %reduce-scatter.2.cloned.1.call-start = ((), (), s32[]{:S(2)}) async-start(), calls=%async_computation.2 | async-start | bytes 2228224 | tf_op jit(solution)/shard_map/reduce_scatter | solution.py:154
  86.8 0.8 copy-start
Sparse Core Ops, SparseCore 0:
  10.2 40.6 all-gather.1
  87.0 60.4 reduce-scatter.1

commit v2 on v1

--- a/solution.py
+++ b/solution.py
@@ -107,13 +107,167 @@
             gk_ref[target] += part[v * BLK : (v + 1) * BLK, :]
 
 
+def axis_bits(count):
+    return count.bit_length() - 1
+
+
+def relative(me, r, bits):
+    where = me
+    for b in range(bits):
+        if (r >> b) & 1:
+            where = where + (1 - 2 * ((me // 2**b) % 2)) * 2**b
+    return where
+
+
+def low_bit(r, bits):
+    return bits if r == 0 else (r & -r).bit_length() - 1
+
+
+def greet(me, bits):
+    barrier = pltpu.get_barrier_semaphore()
+    for b in range(bits):
+        pl.semaphore_signal(
+            barrier,
+            inc=1,
+            device_id={"ctx": relative(me, 2**b, bits)},
+            device_id_type=pl.DeviceIdType.MESH,
+        )
+    pl.semaphore_wait(barrier, bits)
+
+
+def gather_kernel(count, keys_ref, all_ref, send_sem, recv_sem, own_sem):
+    me = lax.axis_index("ctx")
+    bits = axis_bits(count)
+    own = pltpu.make_async_copy(keys_ref, all_ref.at[me], own_sem)
+    own.start()
+    greet(me, bits)
+
+    def hop(r, b):
+        where = relative(me, r, bits)
+        return pltpu.make_async_remote_copy(
+            src_ref=keys_ref if r == 0 else all_ref.at[where],
+            dst_ref=all_ref.at[where],
+            send_sem=send_sem.at[r + 2**b],
+            recv_sem=recv_sem.at[r + 2**b],
+            device_id={"ctx": relative(me, 2**b, bits)},
+            device_id_type=pl.DeviceIdType.MESH,
+        )
+
+    def landed(r):
+        where = relative(me, r, bits)
+        return pltpu.make_async_remote_copy(
+            src_ref=all_ref.at[where],
+            dst_ref=all_ref.at[where],
+            send_sem=send_sem.at[r],
+            recv_sem=recv_sem.at[r],
+            device_id={"ctx": relative(me, 2 ** low_bit(r, bits), bits)},
+            device_id_type=pl.DeviceIdType.MESH,
+        )
+
+    sent = []
+    for b in reversed(range(bits)):
+        sent.append(hop(0, b))
+        sent[-1].start()
+    order = sorted(range(1, count), key=lambda r: (bin(r).count("1"), -low_bit(r, bits)))
+    for r in order:
+        landed(r).wait_recv()
+        for b in reversed(range(low_bit(r, bits))):
+            sent.append(hop(r, b))
+            sent[-1].start()
+    own.wait()
+    for copy in sent:
+        copy.wait_send()
+
+
+def reduce_kernel(count, terms_ref, out_ref, send_buf, wide_buf, recv_buf, send_sem, recv_sem):
+    me = lax.axis_index("ctx")
+    bits = axis_bits(count)
+    greet(me, bits)
+
+    def hop(r):
+        b = low_bit(r, bits)
+        if b == 0:
+            src, dst = terms_ref.at[relative(me, r, bits)], wide_buf.at[r // 2]
+        else:
+            src, dst = send_buf.at[r // 2], recv_buf.at[r // 2]
+        return pltpu.make_async_remote_copy(
+            src_ref=src,
+            dst_ref=dst,
+            send_sem=send_sem.at[r],
+            recv_sem=recv_sem.at[r],
+            device_id={"ctx": relative(me, 2**b, bits)},
+            device_id_type=pl.DeviceIdType.MESH,
+        )
+
+    def total(r):
+        value = terms_ref[relative(me, r, bits)]
+        for b in range(low_bit(r, bits)):
+            hop(r + 2**b).wait_recv()
+            if b == 0:
+                value = value + wide_buf[r // 2]
+            else:
+                value = value + recv_buf[(r + 2**b) // 2].astype(jnp.float32)
+        return value
+
+    def rank(r):
+        b = low_bit(r, bits)
+        return (b, low_bit(r - 2**b, bits), -r)
+
+    order = sorted(range(1, count), key=rank)
+    for r in order:
+        if low_bit(r, bits) > 0:
+            send_buf[r // 2] = total(r).astype(jnp.bfloat16)
+        hop(r).start()
+    out_ref[...] = total(0).astype(jnp.bfloat16)
+    for r in order:
+        hop(r).wait_send()
+
+
+def gather_keys(keys):
+    count = lax.axis_size("ctx")
+    return pl.pallas_call(
+        functools.partial(gather_kernel, count),
+        out_shape=jax.ShapeDtypeStruct((count,) + keys.shape, keys.dtype),
+        in_specs=[pl.BlockSpec(memory_space=pltpu.VMEM)],
+        out_specs=pl.BlockSpec(memory_space=pltpu.VMEM),
+        scratch_shapes=[
+            pltpu.SemaphoreType.DMA((count,)),
+            pltpu.SemaphoreType.DMA((count,)),
+            pltpu.SemaphoreType.DMA,
+        ],
+        compiler_params=pltpu.CompilerParams(
+            collective_id=0, has_side_effects=True, vmem_limit_bytes=32 * 2**20
+        ),
+    )(keys)
+
+
+def reduce_terms(terms):
+    count, rows, width = terms.shape
+    return pl.pallas_call(
+        functools.partial(reduce_kernel, count),
+        out_shape=jax.ShapeDtypeStruct((rows, width), jnp.bfloat16),
+        in_specs=[pl.BlockSpec(memory_space=pltpu.VMEM)],
+        out_specs=pl.BlockSpec(memory_space=pltpu.VMEM),
+        scratch_shapes=[
+            pltpu.VMEM((count // 2, rows, width), jnp.bfloat16),
+            pltpu.VMEM((count // 2, rows, width), jnp.float32),
+            pltpu.VMEM((count // 2, rows, width), jnp.bfloat16),
+            pltpu.SemaphoreType.DMA((count,)),
+            pltpu.SemaphoreType.DMA((count,)),
+        ],
+        compiler_params=pltpu.CompilerParams(
+            collective_id=1, has_side_effects=True, vmem_limit_bytes=52 * 2**20
+        ),
+    )(terms)
+
+
 def shards(queries, head_weights, keys, targets, block_lists):
     width = keys.shape[1]
     heads = queries.shape[1]
     cand = targets.shape[1]
     blocks_here = block_lists.shape[0]
-    everyone = lax.all_gather(keys, "ctx", axis=0, tiled=True)
-    total = everyone.shape[0] // BLK
+    everyone = gather_keys(keys)
+    total = everyone.shape[0] * everyone.shape[1] // BLK
     table = everyone.reshape(total, BLK, width)
     flops = 6 * queries.shape[0] * heads * cand * width
     once = pl.Buffered(1)
@@ -151,10 +305,8 @@
         compiler_params=pltpu.CompilerParams(vmem_limit_bytes=60 * 2**20),
         cost_estimate=pl.CostEstimate(flops=flops, bytes_accessed=10 * 2**20, transcendentals=0),
     )(block_lists, queries, head_weights, table, targets)
-    summed = lax.psum_scatter(
-        grad_table.reshape(-1, width), "ctx", scatter_dimension=0, tiled=True
-    )
-    return (grad_q, grad_w, summed.astype(jnp.bfloat16))
+    grad_keys = reduce_terms(grad_table.reshape((-1,) + keys.shape))
+    return (grad_q, grad_w, grad_keys)
 
 
 def solution(mesh):

time: 156 us -> 74.7 us (0.48)
  waiting for transfers between devices: 101 us -> 0 us
  Pallas kernels: 36 us -> 68.2 us
  between operations: 14 us -> 0.66 us
  local copies, waits for them, and re-layouts: 2.99 us -> 5.49 us
    reduce_scatter x1 -> x0, waiting for transfers between devices: 59.1 us -> none  [shards(): lax.psum_scatter(grad_table.reshape(-1, width), 'ctx', scatter_dimension=...]
    all_gather x1 -> x0, waiting for transfers between devices: 41.4 us -> none  [shards(): everyone = lax.all_gather(keys, 'ctx', axis=0, tiled=True)]
    pallas_call x0 -> x2, Pallas kernels: none -> 32.2 us  [the longest x1 16.3 us: gather_keys(): pl.pallas_call(functools.partial(gather_kernel, count), out_shape=jax.Sha...]
    unnamed x4 -> x7, local copies, waits for them, and re-layouts: 2.99 us -> 5.49 us
  transfers between devices with their start and end apart: 2 -> 0, of which waited for: 2 -> 0; matrix products, arithmetic and copies ran while one was open for 1% -> 0% of each run, Pallas kernels for 0% -> 0%
where the time goes in v2:
time: 74.7 us; the launch traced here: 74.4 us
  Pallas kernels  68.2 us (91%)
  local copies, waits for them, and re-layouts  5.49 us (7%)
    pallas_call x1, Pallas kernels, shards(): pl.pallas_call(compute_kernel, grid_spec=pltpu.PrefetchScalarGridSpec(num...  36 us
    pallas_call x1, Pallas kernels, gather_keys(): pl.pallas_call(functools.partial(gather_kernel, count), out_shape=jax.Sha...  16.3 us
    pallas_call x1, Pallas kernels, reduce_terms(): pl.pallas_call(functools.partial(reduce_kernel, count), out_shape=jax.Sha...  16 us
    unnamed x7, local copies, waits for them, and re-layouts  5.49 us

profile of v2, /device:TPU:0, one launch (start us, length us, event | category | flops | bytes accessed | tf_op | source)
XLA Modules:
  0.0 74.4 jit_solution(10185014179510536691)
XLA Ops:
  0.6 1.5 %copy.8.w_ref = f32[128,64]{1,0:T(8,128)} copy(f32[128,64]{0,1:T(8,128)} %param.6) | data formatting | bytes 65536 | tf_op args[1]
  2.1 0.0 copy-start.1
  2.1 0.8 %copy-done.1 = bf16[256,128]{1,0:T(8,128)(2,1)S(1)} copy-done((bf16[256,128]{1,0:T(8,128)(2,1)S(1)}, bf16[256,128]{1,0:T(8,128)(2,1)}, u32[]{:S(2)}) %copy-start.1) | copy-done | bytes 65560
  3.0 16.3 %shard_map.76 = bf16[16,256,128]{2,1,0:T(8,128)(2,1)S(1)} custom-call(bf16[256,128]{1,0:T(8,128)(2,1)S(1)} %copy-done.1), custom_call_target="tpu_custom_call" | custom-call | tf_op jit(solution)/shard_map/pallas_call | solution.py:228
  19.3 0.0 copy-start
  19.3 1.0 %copy-done = bf16[16,256,128]{2,1,0:T(8,128)(2,1)} copy-done((bf16[16,256,128]{2,1,0:T(8,128)(2,1)}, bf16[16,256,128]{2,1,0:T(8,128)(2,1)S(1)}, u32[]{:S(2)}) %copy-start) | copy-done | bytes 1048600
  20.3 36.0 %shard_map.77 = (bf16[128,64,128]{2,1,0:T(8,128)(2,1)}, f32[128,64]{1,0:T(8,128)}, f32[64,64,128]{2,1,0:T(8,128)}) custom-call(s32[2,32]{1,0:T(2,128)} %lists.1, bf16[128,64,128]{2,1,0:T(8,128)(2,1)} %q_ref.1, f32[128,64]{1,0:T(8,128)} %copy.8.w_ref, bf16[64,64,128]{2,1,0:T(8,128)(2,1)} %bitcast.2, f32[128,2048]{1,0:T(8,128)} %targets_ref.1), custom_call_target="tpu_custom_call" | custom-call | flops 12884901888 | bytes 10485760 | tf_op jit(solution)/shard_map/pallas_call | solution.py:274
  56.2 1.5 %copy.9 = f32[128,64]{0,1:T(8,128)} copy(f32[128,64]{1,0:T(8,128)} %get-tuple-element.10) | data formatting | bytes 65536
  57.8 16.0 %shard_map.78 = bf16[256,128]{1,0:T(8,128)(2,1)S(1)} custom-call(f32[16,256,128]{2,1,0:T(8,128)} %bitcast.3), custom_call_target="tpu_custom_call" | custom-call | tf_op jit(solution)/shard_map/pallas_call | solution.py:246
  73.7 0.6 copy.11
Async XLA Ops:
  2.1 0.8 %copy-start.1 = (bf16[256,128]{1,0:T(8,128)(2,1)S(1)}, bf16[256,128]{1,0:T(8,128)(2,1)}, u32[]{:S(2)}) copy-start(bf16[256,128]{1,0:T(8,128)(2,1)} %keys_ref.1) | copy-start | bytes 196612
  19.3 1.0 %copy-start = (bf16[16,256,128]{2,1,0:T(8,128)(2,1)}, bf16[16,256,128]{2,1,0:T(8,128)(2,1)S(1)}, u32[]{:S(2)}) copy-start(bf16[16,256,128]{2,1,0:T(8,128)(2,1)S(1)} %shard_map.76) | copy-start | bytes 3145732

commit v3 on v2

--- a/solution.py
+++ b/solution.py
@@ -18,7 +18,7 @@
 
 def compute_kernel(
     lists, q_ref, w_ref, table_ref, targets_ref, gq_ref, gw_ref, gk_ref,
-    k_scr, kt_scr, s_scr, wb_scr, idx_scr, g_scr, gkt_scr,
+    k_scr, kt_scr, s_scr, wb_scr, idx_scr, g_scr, gkt_scr, w_scr, gw_scr,
 ):
     c = pl.program_id(0)
     tokens, heads, width = q_ref.shape
@@ -29,6 +29,7 @@
     @pl.when(c == 0)
     def _():
         gk_ref[...] = jnp.zeros_like(gk_ref)
+        w_scr[...] = w_ref[...].T * inv_root
 
     for e in range(entries):
         source = jnp.maximum(lists[c, e], 0)
@@ -38,7 +39,7 @@
 
     for t0 in range(0, tokens, 8):
         wb_scr[t0 : t0 + 8] = jnp.broadcast_to(
-            (w_ref[t0 : t0 + 8, :] * inv_root)[:, :, None], (8, heads, width)
+            w_scr[pl.ds(c * tokens + t0, 8), :][:, :, None], (8, heads, width)
         )
 
     def forward(i, carry):
@@ -95,7 +96,7 @@
             )
         gq = gq.reshape(TB, heads, width)
         gq_ref[pl.ds(t0, TB)] = (gq * wb).astype(jnp.bfloat16)
-        gw_ref[pl.ds(t0, TB), :] = jnp.sum(gq * q, axis=2) * inv_root
+        gw_scr[pl.ds(c * tokens + t0, TB), :] = jnp.sum(gq * q, axis=2) * inv_root
         return carry
 
     lax.fori_loop(0, tokens // TB, backward, 0)
@@ -105,6 +106,10 @@
         for v in range(2):
             target = jnp.maximum(lists[c, u // BLK + v], 0)
             gk_ref[target] += part[v * BLK : (v + 1) * BLK, :]
+
+    @pl.when(c == pl.num_programs(0) - 1)
+    def _():
+        gw_ref[...] = gw_scr[...].T
 
 
 def axis_bits(count):
@@ -228,8 +233,8 @@
     return pl.pallas_call(
         functools.partial(gather_kernel, count),
         out_shape=jax.ShapeDtypeStruct((count,) + keys.shape, keys.dtype),
-        in_specs=[pl.BlockSpec(memory_space=pltpu.VMEM)],
-        out_specs=pl.BlockSpec(memory_space=pltpu.VMEM),
+        in_specs=[pl.BlockSpec(memory_space=pltpu.HBM)],
+        out_specs=pl.BlockSpec(memory_space=pltpu.HBM),
         scratch_shapes=[
             pltpu.SemaphoreType.DMA((count,)),
             pltpu.SemaphoreType.DMA((count,)),
@@ -261,30 +266,26 @@
     )(terms)
 
 
-def shards(queries, head_weights, keys, targets, block_lists):
-    width = keys.shape[1]
-    heads = queries.shape[1]
+def local_grads(queries, head_weights, table, targets, block_lists):
+    rows, heads, width = queries.shape
     cand = targets.shape[1]
-    blocks_here = block_lists.shape[0]
-    everyone = gather_keys(keys)
-    total = everyone.shape[0] * everyone.shape[1] // BLK
-    table = everyone.reshape(total, BLK, width)
-    flops = 6 * queries.shape[0] * heads * cand * width
+    total = table.shape[0]
+    flops = 6 * rows * heads * cand * width
     once = pl.Buffered(1)
-    grad_q, grad_w, grad_table = pl.pallas_call(
+    return pl.pallas_call(
         compute_kernel,
         grid_spec=pltpu.PrefetchScalarGridSpec(
             num_scalar_prefetch=1,
-            grid=(blocks_here,),
+            grid=(block_lists.shape[0],),
             in_specs=[
                 pl.BlockSpec((BLK, heads, width), lambda c, lists: (c, 0, 0)),
-                pl.BlockSpec((BLK, heads), lambda c, lists: (c, 0)),
+                pl.BlockSpec((heads, rows), lambda c, lists: (0, 0)),
                 pl.BlockSpec((total, BLK, width), lambda c, lists: (0, 0, 0), pipeline_mode=once),
                 pl.BlockSpec((BLK, cand), lambda c, lists: (c, 0)),
             ],
             out_specs=[
                 pl.BlockSpec((BLK, heads, width), lambda c, lists: (c, 0, 0)),
-                pl.BlockSpec((BLK, heads), lambda c, lists: (c, 0)),
+                pl.BlockSpec((heads, rows), lambda c, lists: (0, 0)),
                 pl.BlockSpec((total, BLK, width), lambda c, lists: (0, 0, 0), pipeline_mode=once),
             ],
             scratch_shapes=[
@@ -295,18 +296,25 @@
                 pltpu.VMEM((BLK, cand), jnp.float32),
                 pltpu.VMEM((BLK, cand), jnp.float32),
                 pltpu.VMEM((width, cand), jnp.float32),
+                pltpu.VMEM((rows, heads), jnp.float32),
+                pltpu.VMEM((rows, heads), jnp.float32),
             ],
         ),
         out_shape=[
             jax.ShapeDtypeStruct(queries.shape, jnp.bfloat16),
-            jax.ShapeDtypeStruct(head_weights.shape, jnp.float32),
+            jax.ShapeDtypeStruct((heads, rows), jnp.float32),
             jax.ShapeDtypeStruct((total, BLK, width), jnp.float32),
         ],
         compiler_params=pltpu.CompilerParams(vmem_limit_bytes=60 * 2**20),
         cost_estimate=pl.CostEstimate(flops=flops, bytes_accessed=10 * 2**20, transcendentals=0),
-    )(block_lists, queries, head_weights, table, targets)
+    )(block_lists, queries, head_weights.T, table, targets)
+
+
+def shards(queries, head_weights, keys, targets, block_lists):
+    table = gather_keys(keys).reshape(-1, BLK, keys.shape[1])
+    grad_q, grad_w, grad_table = local_grads(queries, head_weights, table, targets, block_lists)
     grad_keys = reduce_terms(grad_table.reshape((-1,) + keys.shape))
-    return (grad_q, grad_w, grad_keys)
+    return (grad_q, grad_w.T, grad_keys)
 
 
 def solution(mesh):

time: 74.7 us -> 71.7 us (0.960)
  local copies, waits for them, and re-layouts: 5.49 us -> 2.46 us
    unnamed x7 -> x5, local copies, waits for them, and re-layouts: 5.49 us -> 2.46 us
where the time goes in v3:
time: 71.7 us; the launch traced here: 71.5 us
  Pallas kernels  68.4 us (95%)
  local copies, waits for them, and re-layouts  2.46 us (3%)
    pallas_call x1, Pallas kernels, local_grads(): pl.pallas_call(compute_kernel, grid_spec=pltpu.PrefetchScalarGridSpec(num...  36.1 us
    pallas_call x1, Pallas kernels, gather_keys(): pl.pallas_call(functools.partial(gather_kernel, count), out_shape=jax.Sha...  16.3 us
    pallas_call x1, Pallas kernels, reduce_terms(): pl.pallas_call(functools.partial(reduce_kernel, count), out_shape=jax.Sha...  16 us
    unnamed x5, local copies, waits for them, and re-layouts  2.46 us

profile of v3, /device:TPU:0, one launch (start us, length us, event | category | flops | bytes accessed | tf_op | source)
XLA Modules:
  0.0 71.5 jit_solution(11537573011293801960)
XLA Ops:
  0.6 0.0 copy-start.1
  0.6 0.8 %copy-done.1 = bf16[256,128]{1,0:T(8,128)(2,1)S(1)} copy-done((bf16[256,128]{1,0:T(8,128)(2,1)S(1)}, bf16[256,128]{1,0:T(8,128)(2,1)}, u32[]{:S(2)}) %copy-start.1) | copy-done | bytes 65560
  1.5 16.3 %shard_map.76 = bf16[16,256,128]{2,1,0:T(8,128)(2,1)S(1)} custom-call(bf16[256,128]{1,0:T(8,128)(2,1)S(1)} %copy-done.1), custom_call_target="tpu_custom_call" | custom-call | tf_op jit(solution)/shard_map/pallas_call | solution.py:233
  17.8 0.0 copy-start
  17.8 1.0 %copy-done = bf16[16,256,128]{2,1,0:T(8,128)(2,1)} copy-done((bf16[16,256,128]{2,1,0:T(8,128)(2,1)}, bf16[16,256,128]{2,1,0:T(8,128)(2,1)S(1)}, u32[]{:S(2)}) %copy-start) | copy-done | bytes 1048600
  18.8 36.1 %shard_map.77 = (bf16[128,64,128]{2,1,0:T(8,128)(2,1)}, f32[64,128]{1,0:T(8,128)}, f32[64,64,128]{2,1,0:T(8,128)}) custom-call(s32[2,32]{1,0:T(2,128)} %lists.1, bf16[128,64,128]{2,1,0:T(8,128)(2,1)} %q_ref.1, f32[64,128]{1,0:T(8,128)} %bitcast.6, bf16[64,64,128]{2,1,0:T(8,128)(2,1)} %bitcast.4, f32[128,2048]{1,0:T(8,128)} %targets_ref.1), custom_call_target="tpu_custom_call" | custom-call | flops 12884901888 | bytes 10485760 | tf_op jit(solution)/shard_map/pallas_call | solution.py:275
  54.9 16.0 %shard_map.78 = bf16[256,128]{1,0:T(8,128)(2,1)S(1)} custom-call(f32[16,256,128]{2,1,0:T(8,128)} %bitcast.5), custom_call_target="tpu_custom_call" | custom-call | tf_op jit(solution)/shard_map/pallas_call | solution.py:251
  70.9 0.6 copy.9
Async XLA Ops:
  0.6 0.8 %copy-start.1 = (bf16[256,128]{1,0:T(8,128)(2,1)S(1)}, bf16[256,128]{1,0:T(8,128)(2,1)}, u32[]{:S(2)}) copy-start(bf16[256,128]{1,0:T(8,128)(2,1)} %keys_ref.1) | copy-start | bytes 196612
  17.8 1.0 %copy-start = (bf16[16,256,128]{2,1,0:T(8,128)(2,1)}, bf16[16,256,128]{2,1,0:T(8,128)(2,1)S(1)}, u32[]{:S(2)}) copy-start(bf16[16,256,128]{2,1,0:T(8,128)(2,1)S(1)} %shard_map.76) | copy-start | bytes 3145732

commit v4 on v3

--- a/solution.py
+++ b/solution.py
@@ -11,9 +11,9 @@
 BLK = 64
 LOSS_WEIGHT = 256.0
 FAR = 2**30
-UC = 256
-TF = 8
-TB = 8
+UC = 512
+TF = 16
+TB = 16
 
 
 def compute_kernel(

time: 71.7 us -> 69.2 us (0.965)
  Pallas kernels: 68.4 us -> 65.9 us
    pallas_call x1, Pallas kernels: 36.1 us -> 33.6 us  [local_grads(): pl.pallas_call(compute_kernel, grid_spec=pltpu.PrefetchScalarGridSpec(num...]
where the time goes in v4:
time: 69.2 us; the launch traced here: 69 us
  Pallas kernels  65.9 us (95%)
  local copies, waits for them, and re-layouts  2.46 us (4%)
    pallas_call x1, Pallas kernels, local_grads(): pl.pallas_call(compute_kernel, grid_spec=pltpu.PrefetchScalarGridSpec(num...  33.6 us
    pallas_call x1, Pallas kernels, gather_keys(): pl.pallas_call(functools.partial(gather_kernel, count), out_shape=jax.Sha...  16.3 us
    pallas_call x1, Pallas kernels, reduce_terms(): pl.pallas_call(functools.partial(reduce_kernel, count), out_shape=jax.Sha...  16 us
    unnamed x5, local copies, waits for them, and re-layouts  2.46 us

profile of v4, /device:TPU:0, one launch (start us, length us, event | category | flops | bytes accessed | tf_op | source)
XLA Modules:
  0.0 69.0 jit_solution(1842005738243984346)
XLA Ops:
  0.6 0.0 copy-start.1
  0.6 0.8 %copy-done.1 = bf16[256,128]{1,0:T(8,128)(2,1)S(1)} copy-done((bf16[256,128]{1,0:T(8,128)(2,1)S(1)}, bf16[256,128]{1,0:T(8,128)(2,1)}, u32[]{:S(2)}) %copy-start.1) | copy-done | bytes 65560
  1.5 16.3 %shard_map.76 = bf16[16,256,128]{2,1,0:T(8,128)(2,1)S(1)} custom-call(bf16[256,128]{1,0:T(8,128)(2,1)S(1)} %copy-done.1), custom_call_target="tpu_custom_call" | custom-call | tf_op jit(solution)/shard_map/pallas_call | solution.py:233
  17.8 0.0 copy-start
  17.8 1.0 %copy-done = bf16[16,256,128]{2,1,0:T(8,128)(2,1)} copy-done((bf16[16,256,128]{2,1,0:T(8,128)(2,1)}, bf16[16,256,128]{2,1,0:T(8,128)(2,1)S(1)}, u32[]{:S(2)}) %copy-start) | copy-done | bytes 1048600
  18.8 33.6 %shard_map.77 = (bf16[128,64,128]{2,1,0:T(8,128)(2,1)}, f32[64,128]{1,0:T(8,128)}, f32[64,64,128]{2,1,0:T(8,128)}) custom-call(s32[2,32]{1,0:T(2,128)} %lists.1, bf16[128,64,128]{2,1,0:T(8,128)(2,1)} %q_ref.1, f32[64,128]{1,0:T(8,128)} %bitcast.6, bf16[64,64,128]{2,1,0:T(8,128)(2,1)} %bitcast.4, f32[128,2048]{1,0:T(8,128)} %targets_ref.1), custom_call_target="tpu_custom_call" | custom-call | flops 12884901888 | bytes 10485760 | tf_op jit(solution)/shard_map/pallas_call | solution.py:275
  52.4 16.0 %shard_map.78 = bf16[256,128]{1,0:T(8,128)(2,1)S(1)} custom-call(f32[16,256,128]{2,1,0:T(8,128)} %bitcast.5), custom_call_target="tpu_custom_call" | custom-call | tf_op jit(solution)/shard_map/pallas_call | solution.py:251
  68.4 0.6 copy.9
Async XLA Ops:
  0.6 0.8 %copy-start.1 = (bf16[256,128]{1,0:T(8,128)(2,1)S(1)}, bf16[256,128]{1,0:T(8,128)(2,1)}, u32[]{:S(2)}) copy-start(bf16[256,128]{1,0:T(8,128)(2,1)} %keys_ref.1) | copy-start | bytes 196612
  17.8 1.0 %copy-start = (bf16[16,256,128]{2,1,0:T(8,128)(2,1)}, bf16[16,256,128]{2,1,0:T(8,128)(2,1)S(1)}, u32[]{:S(2)}) copy-start(bf16[16,256,128]{2,1,0:T(8,128)(2,1)S(1)} %shard_map.76) | copy-start | bytes 3145732

commit v5 on v3

--- a/solution.py
+++ b/solution.py
@@ -12,8 +12,8 @@
 LOSS_WEIGHT = 256.0
 FAR = 2**30
 UC = 256
-TF = 8
-TB = 8
+TF = 32
+TB = 32
 
 
 def compute_kernel(

time: 71.7 us -> 67 us (0.934)
  Pallas kernels: 68.4 us -> 63.7 us
    pallas_call x1, Pallas kernels: 36.1 us -> 31.4 us  [local_grads(): pl.pallas_call(compute_kernel, grid_spec=pltpu.PrefetchScalarGridSpec(num...]
where the time goes in v5:
time: 67 us; the launch traced here: 66.8 us
  Pallas kernels  63.7 us (95%)
  local copies, waits for them, and re-layouts  2.46 us (4%)
    pallas_call x1, Pallas kernels, local_grads(): pl.pallas_call(compute_kernel, grid_spec=pltpu.PrefetchScalarGridSpec(num...  31.4 us
    pallas_call x1, Pallas kernels, gather_keys(): pl.pallas_call(functools.partial(gather_kernel, count), out_shape=jax.Sha...  16.3 us
    pallas_call x1, Pallas kernels, reduce_terms(): pl.pallas_call(functools.partial(reduce_kernel, count), out_shape=jax.Sha...  16 us
    unnamed x5, local copies, waits for them, and re-layouts  2.46 us

profile of v5, /device:TPU:0, one launch (start us, length us, event | category | flops | bytes accessed | tf_op | source)
XLA Modules:
  0.0 66.8 jit_solution(5638973506123429626)
XLA Ops:
  0.6 0.0 copy-start.1
  0.6 0.8 %copy-done.1 = bf16[256,128]{1,0:T(8,128)(2,1)S(1)} copy-done((bf16[256,128]{1,0:T(8,128)(2,1)S(1)}, bf16[256,128]{1,0:T(8,128)(2,1)}, u32[]{:S(2)}) %copy-start.1) | copy-done | bytes 65560
  1.5 16.3 %shard_map.76 = bf16[16,256,128]{2,1,0:T(8,128)(2,1)S(1)} custom-call(bf16[256,128]{1,0:T(8,128)(2,1)S(1)} %copy-done.1), custom_call_target="tpu_custom_call" | custom-call | tf_op jit(solution)/shard_map/pallas_call | solution.py:233
  17.8 0.0 copy-start
  17.8 1.0 %copy-done = bf16[16,256,128]{2,1,0:T(8,128)(2,1)} copy-done((bf16[16,256,128]{2,1,0:T(8,128)(2,1)}, bf16[16,256,128]{2,1,0:T(8,128)(2,1)S(1)}, u32[]{:S(2)}) %copy-start) | copy-done | bytes 1048600
  18.8 31.4 %shard_map.77 = (bf16[128,64,128]{2,1,0:T(8,128)(2,1)}, f32[64,128]{1,0:T(8,128)}, f32[64,64,128]{2,1,0:T(8,128)}) custom-call(s32[2,32]{1,0:T(2,128)} %lists.1, bf16[128,64,128]{2,1,0:T(8,128)(2,1)} %q_ref.1, f32[64,128]{1,0:T(8,128)} %bitcast.6, bf16[64,64,128]{2,1,0:T(8,128)(2,1)} %bitcast.4, f32[128,2048]{1,0:T(8,128)} %targets_ref.1), custom_call_target="tpu_custom_call" | custom-call | flops 12884901888 | bytes 10485760 | tf_op jit(solution)/shard_map/pallas_call | solution.py:275
  50.2 16.0 %shard_map.78 = bf16[256,128]{1,0:T(8,128)(2,1)S(1)} custom-call(f32[16,256,128]{2,1,0:T(8,128)} %bitcast.5), custom_call_target="tpu_custom_call" | custom-call | tf_op jit(solution)/shard_map/pallas_call | solution.py:251
  66.2 0.6 copy.9
Async XLA Ops:
  0.6 0.8 %copy-start.1 = (bf16[256,128]{1,0:T(8,128)(2,1)S(1)}, bf16[256,128]{1,0:T(8,128)(2,1)}, u32[]{:S(2)}) copy-start(bf16[256,128]{1,0:T(8,128)(2,1)} %keys_ref.1) | copy-start | bytes 196612
  17.8 1.0 %copy-start = (bf16[16,256,128]{2,1,0:T(8,128)(2,1)}, bf16[16,256,128]{2,1,0:T(8,128)(2,1)S(1)}, u32[]{:S(2)}) copy-start(bf16[16,256,128]{2,1,0:T(8,128)(2,1)S(1)} %shard_map.76) | copy-start | bytes 3145732
